TPU v7x, 256 devices: a whole 4x4x8 slice. The times are simulated.
256 devices in a mesh: ctx: 128 (over y, x_lo, z, core), head: 2 (over x_hi).
Axes of the slice: x: 4 (x_hi: 2, x_lo: 2; x = x_hi * 2 + x_lo), y: 4, z: 8, core: 2. Of those that a mesh axis runs over, the one named last changes fastest.
Arguments:
- q_raw: bfloat16 [32768, 4096], P('ctx', 'head'), may hold values from -8 to 8
- k_raw: bfloat16 [32768, 4096], P('ctx', 'head'), may hold values from -8 to 8
- v_raw: bfloat16 [32768, 4096], P('ctx', 'head'), may hold values from -8 to 8
- g_raw: bfloat16 [32768, 4096], P('ctx', 'head'), may hold values from -6 to 6
- short_filters: float32 [4, 3, 4096], P(None, None, 'head'), may hold values from 0.2 to 1
- long_filter: float32 [7, 4096], P(None, 'head'), may hold values from -2 to 2
- out_gain: float32 [4096], P('head'), may hold values from 0.25 to 1.75
- block_lists: int32 [256, 7], replicated, may hold values from -1 to 255, as said below
Outputs:
- normed: bfloat16 [32768, 4096], P('ctx', 'head')
Inputs may be any that keep to these rules, and one draw needn't show every extreme that they name: `block_lists`: row i holds in slot t < 3 the block i - t, or -1 where i - t < 0. In slot 3 + s it holds either -1 or p + s * 64, the latter only where that is at most i - 3, with one offset p of 0 to 60 for the whole array. Each row keeps or drops each such global entry by its own drawn choice. The last row keeps all of them.
All inputs are finite; a program needn't handle non-finite values.
Results may differ from a plain program's by a relative error of at most 0.0086.
Values may be sent and summed in bfloat16 or wider, within the bound.
A program may use at most 128 MiB of HBM per device.

v0:
```python
import functools
import math

import jax
import jax.numpy as jnp
from jax import lax
from jax.experimental import pallas as pl
from jax.experimental.pallas import tpu as pltpu
from jax.sharding import PartitionSpec as P

D = 4096
HS = 128
BLK = 128
BAND = 3
NGLOB = 4
TAPS = 3
TAPS_LONG = 7
ROWS = 256
HEADS_HERE = 16
HALF = 8
HALO = 16
LAG = 3
EARLY = 12
BATCH = 4
WIDE = 512
COLUMNS = 4
GROUP = 1
PART = 64
MESH = pl.DeviceIdType.MESH
F32 = jnp.float32
BF16 = jnp.bfloat16
VMEM = pltpu.VMEM
MIB = 1024 * 1024


def taps_of(ext, weights, count):
    total = weights[0:1] * ext
    for s in range(1, count):
        total = total + weights[s : s + 1] * pltpu.roll(ext, s, 0)
    return total


def features_kernel(
    parity_ref, q_ref, k_ref, v_ref, g_ref, sf_in, lf_in,
    qf_ref, kv_ref, cand_ref, halo, held, sf_ref, lf_ref, send_sem, recv_sem, load_sem, tap_sem,
):
    me = lax.axis_index("ctx")
    last = lax.axis_size("ctx") - 1
    streams = (q_ref, k_ref, v_ref, g_ref)
    barrier = pltpu.get_barrier_semaphore()

    for other in ((me + last) % (last + 1), (me + 1) % (last + 1)):
        pl.semaphore_signal(barrier, inc=1, device_id={"ctx": other}, device_id_type=MESH)

    def load(i, c):
        span = pl.ds(pl.multiple_of(c * WIDE, WIDE), WIDE)
        return pltpu.make_async_copy(
            streams[i].at[:, span], held.at[i, :, span], load_sem.at[i, c]
        )

    taps = [
        pltpu.make_async_copy(sf_in, sf_ref, tap_sem.at[0]),
        pltpu.make_async_copy(lf_in, lf_ref, tap_sem.at[1]),
    ]
    for copy in taps:
        copy.start()
    for c in range(COLUMNS):
        for i in range(4):
            load(i, c).start()
    pl.semaphore_wait(barrier, 2)

    def tail_copy(i):
        return pltpu.make_async_remote_copy(
            src_ref=streams[i].at[pl.ds(ROWS - HALO, HALO)],
            dst_ref=halo.at[i],
            send_sem=send_sem.at[i],
            recv_sem=recv_sem.at[i],
            device_id={"ctx": me + 1},
            device_id_type=MESH,
        )

    @pl.when(me < last)
    def _():
        for i in range(4):
            tail_copy(i).start()

    @pl.when(me == 0)
    def _():
        halo[...] = jnp.zeros_like(halo)

    def part(h, r):
        cols = pl.ds(pl.multiple_of(h * HS, HS), HS)

        def extended(i):
            if r == 0:
                before = halo[i, :, cols].astype(F32)
                return jnp.concatenate([before, held[i, 0:PART, cols].astype(F32)], 0)
            return held[i, r * PART - HALO : (r + 1) * PART, cols].astype(F32)

        feats = [taps_of(extended(i), sf_ref[:, i, cols], TAPS) for i in range(4)]
        values = taps_of(feats[3] * feats[2], lf_ref[:, cols], TAPS_LONG)
        qf_ref[h, r * PART : (r + 1) * PART, :] = feats[0][HALO:].astype(BF16)
        low = r * PART % BLK
        kv_ref[r * PART // BLK, h, 0, low : low + PART, :] = feats[1][HALO:].astype(BF16)
        kv_ref[r * PART // BLK, h, 1, low : low + PART, :] = values[HALO:].astype(BF16)

    for copy in taps:
        copy.wait()

    @pl.loop(0, COLUMNS)
    def _(c):
        for i in range(4):
            load(i, c).wait()

        @pl.loop(0, HEADS_HERE // COLUMNS)
        def _(n):
            for r in range(1, ROWS // PART):
                part(c * (HEADS_HERE // COLUMNS) + n, r)

    @pl.when(me > 0)
    def _():
        for i in range(4):
            tail_copy(i).wait_recv()

    parity = parity_ref[0]

    @pl.loop(0, HEADS_HERE)
    def _(h):
        part(h, 0)
        cand_ref[h] = kv_ref[parity, h]

    @pl.when(me < last)
    def _():
        for i in range(4):
            tail_copy(i).wait_send()


def features(parity, q_raw, k_raw, v_raw, g_raw, short_filters, long_filter):
    vm = pl.BlockSpec(memory_space=VMEM)
    return pl.pallas_call(
        features_kernel,
        out_shape=(
            jax.ShapeDtypeStruct((HEADS_HERE, ROWS, HS), BF16),
            jax.ShapeDtypeStruct((2, HEADS_HERE, 2, BLK, HS), BF16),
            jax.ShapeDtypeStruct((HEADS_HERE, 2, BLK, HS), BF16),
        ),
        in_specs=[pl.BlockSpec(memory_space=pltpu.SMEM)] + [pl.BlockSpec(memory_space=pl.ANY)] * 6,
        out_specs=(vm, vm, vm),
        scratch_shapes=[
            VMEM((4, HALO, HEADS_HERE * HS), BF16),
            VMEM((4, ROWS, HEADS_HERE * HS), BF16),
            VMEM((TAPS, 4, HEADS_HERE * HS), F32),
            VMEM((TAPS_LONG, HEADS_HERE * HS), F32),
            pltpu.SemaphoreType.DMA((4,)),
            pltpu.SemaphoreType.DMA((4,)),
            pltpu.SemaphoreType.DMA((4, COLUMNS)),
            pltpu.SemaphoreType.DMA((2,)),
        ],
        compiler_params=pltpu.CompilerParams(
            collective_id=0, has_side_effects=True, vmem_limit_bytes=56 * MIB
        ),
        name="features",
    )(parity, q_raw, k_raw, v_raw, g_raw, short_filters, long_filter)


def exchange_kernel(source, kv_ref, cand_ref, band_ref, glob_ref, send_sem, recv_sem, band_send, band_recv, fill_sem):
    x0, z0, c0 = source // 16, source // 2 % 8, source % 2
    me = lax.axis_index("ctx")
    last = lax.axis_size("ctx") - 1
    core = me % 2
    z = me // 2 % 8
    x = me // 16 % 2
    y = me // 32
    steps = (z0 - z + 8) % 8

    def at(yy, xx, zz, cc):
        return ((yy * 2 + xx) * 8 + zz) * 2 + cc

    x_other = at(y, 1 - x, z, core)
    y_up, y_down = at((y + 1) % 4, x, z, core), at((y + 3) % 4, x, z, core)
    sibling = at(y, x, z, 1 - core)
    outer = (me + last + 2 * core) % (last + 1)

    barrier = pltpu.get_barrier_semaphore()
    z_targets = {kind: at(y, x, (z + move) % 8, core) for kind, move in [(6, 7), (7, 1), (8, 5), (9, 2)]}
    z_others = [at(y, x, (z + move) % 8, core) for move in (1, 7, 3, 5, 2, 6)]
    for other in z_others + [x_other, y_up, y_down, sibling, outer]:
        pl.semaphore_signal(barrier, inc=1, device_id={"ctx": other}, device_id_type=MESH)
    pl.semaphore_wait(barrier, 11)

    def band_copy(b):
        return pltpu.make_async_remote_copy(
            src_ref=kv_ref.at[b, pl.ds(0, EARLY)], dst_ref=band_ref.at[b],
            send_sem=band_send.at[b], recv_sem=band_recv.at[b],
            device_id={"ctx": me + 1}, device_id_type=MESH,
        )

    @pl.when(me < last)
    def _():
        for b in range(2):
            band_copy(b).start()

    @pl.when(me == 0)
    def _():
        for b in range(2):
            pltpu.make_async_copy(
                cand_ref.at[pl.ds(0, EARLY)], band_ref.at[b], band_recv.at[b]
            ).start()

    main = x == (x0 + core) % 2
    at_source = (x == x0) & (steps == 0)
    mine, theirs = core * HALF, (1 - core) * HALF

    plans = []
    for s in range(NGLOB):
        plane = y == s
        along = plane & main
        z_routes = [
            (8, along & (steps == 0), z_targets[8]),
            (9, along & (steps == 0), z_targets[9]),
            (6, along & ((steps == 0) | (steps == 1) | (steps == 3) | (steps == 6)), z_targets[6]),
            (7, along & (steps == 6), z_targets[7]),
        ]
        over_x = plane & (
            (main & jnp.logical_not((core == 1) & (steps == 0)))
            | (jnp.logical_not(main) & (core == 1) & (steps == 0))
        )
        never = y < 0
        up = [
            (y == 0) | ((y == 1) & (core == 0)),
            (y == 1) | ((y == 2) & (core == 0)),
            y == 2,
            never,
        ][s]
        down = [
            (y == 0) | ((y == 3) & (core == 1)),
            ((y == 1) | (y == 0)) & (core == 1),
            never,
            never,
        ][s]
        needs = y >= s
        owner = plane & at_source & (core == c0)
        near_owner = plane & at_source & (core != c0)
        holds = needs if s != 1 else (needs | ((y == 0) & (core == 1)))
        share = needs & jnp.logical_not(near_owner)
        routes = []
        if s < 3:
            routes += [(2, up, y_up)]
        if s < 2:
            routes += [(3, down, y_down)]
        routes = z_routes + [(1, over_x, x_other)] + routes + [(4, share, sibling)]
        depth = [
            jnp.where(y == 0, 0, jnp.where(y == 2, 2, 1)),
            jnp.where(y == 1, 0, jnp.where(y == 3, 2, 1)),
            jnp.where(y == 2, 0, 1),
            0,
        ][s]
        plans.append((needs, owner, holds, routes, depth * LAG))

    def send(s, h, kind, target):
        return pltpu.make_async_remote_copy(
            src_ref=glob_ref.at[s, pl.ds(h, GROUP)], dst_ref=glob_ref.at[s, pl.ds(h, GROUP)],
            send_sem=send_sem.at[s, kind], recv_sem=recv_sem.at[s, h],
            device_id={"ctx": target}, device_id_type=MESH,
        )

    def sent(s, kind, first):
        span = glob_ref.at[s, pl.ds(first, HALF)]
        return pltpu.make_async_remote_copy(
            src_ref=span, dst_ref=span,
            send_sem=send_sem.at[s, kind], recv_sem=recv_sem.at[s, 0],
            device_id={"ctx": sibling}, device_id_type=MESH,
        )

    for s in range(NGLOB):
        needs, owner, holds, routes, lag = plans[s]

        @pl.when(owner)
        def _():
            @pl.loop(0, HEADS_HERE // GROUP)
            def _(i):
                span = pl.ds(i * GROUP, GROUP)
                pltpu.make_async_copy(
                    cand_ref.at[span], glob_ref.at[s, span], recv_sem.at[s, i * GROUP]
                ).start()

        @pl.when(jnp.logical_not(needs))
        def _():
            span = pl.ds(theirs, HALF)
            pltpu.make_async_copy(cand_ref.at[span], glob_ref.at[s, span], fill_sem.at[s, 0]).start()

        @pl.when(jnp.logical_not(holds))
        def _():
            span = pl.ds(mine, HALF)
            pltpu.make_async_copy(cand_ref.at[span], glob_ref.at[s, span], fill_sem.at[s, 1]).start()

    @pl.loop(0, HALF // GROUP + 2 * LAG)
    def _(t):
        for s in (3, 2, 1, 0):
            needs, owner, holds, routes, lag = plans[s]
            j = t - lag
            turn = (j >= 0) & (j < HALF // GROUP)

            @pl.when(holds & turn)
            def _():
                h = mine + j * GROUP
                send(s, h, 0, sibling).wait_recv()
                for kind, on, target in routes:

                    @pl.when(on)
                    def _():
                        send(s, h, kind, target).start()

            @pl.when(owner & turn)
            def _():
                h = theirs + j * GROUP
                send(s, h, 5, sibling).wait_recv()
                send(s, h, 5, sibling).start()

    for s in range(NGLOB):
        needs, owner, holds, routes, lag = plans[s]

        @pl.when(needs & jnp.logical_not(owner))
        def _():
            @pl.loop(0, HALF // GROUP)
            def _(j):
                send(s, theirs + j * GROUP, 0, sibling).wait_recv()

        @pl.when(owner)
        def _():
            sent(s, 5, theirs).wait_send()

        for kind, on, target in routes:

            @pl.when(on)
            def _():
                sent(s, kind, mine).wait_send()

        @pl.when(jnp.logical_not(needs))
        def _():
            span = pl.ds(theirs, HALF)
            pltpu.make_async_copy(cand_ref.at[span], glob_ref.at[s, span], fill_sem.at[s, 0]).wait()

        @pl.when(jnp.logical_not(holds))
        def _():
            span = pl.ds(mine, HALF)
            pltpu.make_async_copy(cand_ref.at[span], glob_ref.at[s, span], fill_sem.at[s, 1]).wait()

    @pl.when(me < last)
    def _():
        for b in range(2):
            band_copy(b).wait_send()

    for b in range(2):
        band_copy(b).wait_recv()


def exchange(source, kv, cand):
    vm = pl.BlockSpec(memory_space=VMEM)
    hbm = pl.BlockSpec(memory_space=pl.ANY)
    return pl.pallas_call(
        functools.partial(exchange_kernel, source),
        out_shape=(
            jax.ShapeDtypeStruct((2, EARLY, 2, BLK, HS), BF16),
            jax.ShapeDtypeStruct((NGLOB, HEADS_HERE, 2, BLK, HS), BF16),
        ),
        in_specs=[vm, vm],
        out_specs=(hbm, hbm),
        scratch_shapes=[
            pltpu.SemaphoreType.DMA((NGLOB, 10)),
            pltpu.SemaphoreType.DMA((NGLOB, HEADS_HERE)),
            pltpu.SemaphoreType.DMA((2,)),
            pltpu.SemaphoreType.DMA((2,)),
            pltpu.SemaphoreType.DMA((NGLOB, 2)),
        ],
        compiler_params=pltpu.CompilerParams(
            collective_id=2 + source, has_side_effects=True, vmem_limit_bytes=32 * MIB
        ),
        name=f"exchange_{source}",
    )(kv, cand)


def attention_kernel(
    bias_ref, q_ref, kv_ref, early_in, glob_in, gain_ref, out_ref,
    att, square, mine, theirs, band_ref, glob_ref,
    send_sem, recv_sem, early_sem, glob_sem, band_send, band_recv,
):
    me = lax.axis_index("ctx")
    last = lax.axis_size("ctx") - 1
    partner = 1 - lax.axis_index("head")
    barrier = pltpu.get_barrier_semaphore()

    pl.semaphore_signal(barrier, inc=1, device_id={"head": partner}, device_id_type=MESH)
    for other in ((me + last) % (last + 1), (me + 1) % (last + 1)):
        pl.semaphore_signal(barrier, inc=1, device_id={"ctx": other}, device_id_type=MESH)

    def early(g):
        span = pl.ds(g * BATCH, BATCH)
        return pltpu.make_async_copy(early_in.at[:, span], band_ref.at[:, span], early_sem.at[g])

    def globals_of(g):
        span = pl.ds(g * BATCH, BATCH)
        return pltpu.make_async_copy(glob_in.at[:, span], glob_ref.at[:, span], glob_sem.at[g])

    def late(b):
        span = pl.ds(EARLY, HEADS_HERE - EARLY)
        return pltpu.make_async_remote_copy(
            src_ref=kv_ref.at[b, span], dst_ref=band_ref.at[b, span],
            send_sem=band_send.at[b], recv_sem=band_recv.at[b],
            device_id={"ctx": me + 1}, device_id_type=MESH,
        )

    for g in range(HEADS_HERE // BATCH):
        globals_of(g).start()
        if g < EARLY // BATCH:
            early(g).start()
    square[...] = jnp.zeros_like(square)

    @pl.when(me == 0)
    def _():
        for b in range(2):
            span = pl.ds(EARLY, HEADS_HERE - EARLY)
            pltpu.make_async_copy(
                kv_ref.at[b, span], band_ref.at[b, span], band_recv.at[b]
            ).start()

    pl.semaphore_wait(barrier, 3)

    @pl.when(me < last)
    def _():
        for b in range(2):
            late(b).start()


    edge = jnp.where(me == 0, -jnp.inf, 0.0).astype(F32)
    rows = lax.broadcasted_iota(jnp.int32, (BLK, BLK), 0)
    cols = lax.broadcasted_iota(jnp.int32, (BLK, BLK), 1)
    causal = jnp.where(rows >= cols, 0.0, -jnp.inf).astype(F32)
    scale = math.log2(math.e) / math.sqrt(HS)

    def times(a, b):
        return lax.dot_general(a, b, (((1,), (1,)), ((), ())), preferred_element_type=F32)

    def mix(a, b):
        return jnp.dot(a.astype(BF16), b, preferred_element_type=F32)

    @pl.loop(0, HEADS_HERE)
    def _(i):
        g = i // BATCH

        @pl.when(i % BATCH == 0)
        def _():
            globals_of(g).wait()

        @pl.when((i % BATCH == 0) & (i < EARLY))
        def _():
            early(g).wait()

        @pl.when(i == EARLY)
        def _():
            for b in range(2):
                late(b).wait_recv()

        q = q_ref[i]
        halves = [q[:BLK], q[BLK:]]
        wide = times(q, glob_ref[:, i, 0].reshape(NGLOB * BLK, HS))
        near = times(q, band_ref[1, i, 0])
        first = times(q, kv_ref[0, i, 0])
        extra = [times(halves[0], band_ref[0, i, 0]), times(halves[1], kv_ref[1, i, 0])]
        w_wide, w_near, w_first, w_extra, totals = [], [], [], [], []
        for b in range(2):
            span = slice(b * BLK, (b + 1) * BLK)
            scores = [
                near[span] + edge,
                first[span] + causal if b == 0 else first[span],
                extra[b] + (edge if b == 0 else causal),
            ]
            scores += [
                wide[span, s * BLK : (s + 1) * BLK] + bias_ref[b, s] for s in range(NGLOB)
            ]
            top = scores[0]
            for one in scores[1:]:
                top = jnp.maximum(top, one)
            top = jnp.max(top, axis=1, keepdims=True) * scale
            weights = [jnp.exp2(one * scale - top) for one in scores]
            total = weights[0]
            for one in weights[1:]:
                total = total + one
            totals.append(1.0 / jnp.sum(total, axis=1, keepdims=True))
            w_near.append(weights[0])
            w_first.append(weights[1])
            w_extra.append(mix(weights[2], (band_ref if b == 0 else kv_ref)[b, i, 1]))
            w_wide.append(jnp.concatenate(weights[3:], 1))
        blend = mix(jnp.concatenate(w_wide, 0), glob_ref[:, i, 1].reshape(NGLOB * BLK, HS))
        blend = blend + mix(jnp.concatenate(w_near, 0), band_ref[1, i, 1])
        blend = blend + mix(jnp.concatenate(w_first, 0), kv_ref[0, i, 1])
        blend = blend + jnp.concatenate(w_extra, 0)
        value = blend * jnp.concatenate(totals, 0)
        att[i] = value
        square[...] += value * value

    mine[...] = jnp.sum(jnp.transpose(square[...]).reshape(HS // 8, 8, ROWS), axis=0)
    copy = pltpu.make_async_remote_copy(
        src_ref=mine, dst_ref=theirs, send_sem=send_sem, recv_sem=recv_sem,
        device_id={"head": partner}, device_id_type=MESH,
    )
    copy.start()
    copy.wait()

    @pl.when(me < last)
    def _():
        for b in range(2):
            late(b).wait_send()

    energy = jnp.sum(mine[...] + theirs[...], axis=0, keepdims=True) / D
    factor = jnp.broadcast_to(lax.rsqrt(energy + 1e-06), (8, ROWS))
    square[...] = jnp.broadcast_to(jnp.transpose(factor)[:, 0:1], (ROWS, HS))

    @pl.loop(0, HEADS_HERE)
    def _(i):
        span = pl.ds(pl.multiple_of(i * HS, HS), HS)
        out_ref[:, span] = (att[i] * gain_ref[:, span] * square[...]).astype(BF16)


def attention(bias, qf, kv, band, glob, gain):
    vm = pl.BlockSpec(memory_space=VMEM)
    hbm = pl.BlockSpec(memory_space=pl.ANY)
    return pl.pallas_call(
        attention_kernel,
        out_shape=jax.ShapeDtypeStruct((ROWS, HEADS_HERE * HS), BF16),
        in_specs=[pl.BlockSpec(memory_space=pltpu.SMEM), vm, vm, hbm, hbm, vm],
        out_specs=vm,
        scratch_shapes=[
            VMEM((HEADS_HERE, ROWS, HS), F32),
            VMEM((ROWS, HS), F32),
            VMEM((8, ROWS), F32),
            VMEM((8, ROWS), F32),
            VMEM((2, HEADS_HERE, 2, BLK, HS), BF16),
            VMEM((NGLOB, HEADS_HERE, 2, BLK, HS), BF16),
            pltpu.SemaphoreType.DMA,
            pltpu.SemaphoreType.DMA,
            pltpu.SemaphoreType.DMA((EARLY // BATCH,)),
            pltpu.SemaphoreType.DMA((HEADS_HERE // BATCH,)),
            pltpu.SemaphoreType.DMA((2,)),
            pltpu.SemaphoreType.DMA((2,)),
        ],
        compiler_params=pltpu.CompilerParams(
            collective_id=1, has_side_effects=True, vmem_limit_bytes=48 * MIB
        ),
        name="attention",
    )(bias, qf, kv, band, glob, gain)


def per_device(q_raw, k_raw, v_raw, g_raw, short_filters, long_filter, out_gain, block_lists):
    phase = block_lists[block_lists.shape[0] - 1, BAND]
    first = lax.axis_index("ctx") * 2
    own = lax.dynamic_slice_in_dim(block_lists, first, 2, 0)[:, BAND:]
    bias = jnp.where(own >= 0, 0.0, -jnp.inf).astype(F32)
    parity = jnp.reshape(phase & 1, (1,))
    qf, kv, cand = features(
        parity, q_raw, k_raw, v_raw, g_raw, jnp.transpose(short_filters, (1, 0, 2)), long_filter
    )
    band, glob = lax.switch(
        lax.shift_right_logical(phase, 1), [functools.partial(exchange, source) for source in range(31)], kv, cand
    )
    return attention(bias, qf, kv, band, glob, out_gain[None, :])


def solution(mesh):
    placed = (
        P("ctx", "head"),
        P("ctx", "head"),
        P("ctx", "head"),
        P("ctx", "head"),
        P(None, None, "head"),
        P(None, "head"),
        P("head"),
        P(),
    )
    return jax.shard_map(
        per_device, mesh=mesh, in_specs=placed, out_specs=P("ctx", "head"), check_vma=False
    )
```

profile of v0, /device:TPU:24, one launch (start us, length us, event | category | flops | bytes accessed | tf_op | source)
XLA Modules:
  0.0 82.3 jit_solution(3703049754519534286)
XLA Ops:
  0.0 1.3 %slice.7 = s32[1,1]{0,1:T(1,128)} slice(s32[256,7]{0,1:T(8,128)} %param.46), slice={[255:256], [3:4]} | slice | bytes 8 | tf_op jit(solution)/shard_map/slice | solution.py:555
  1.9 14.2 %features.1 = (bf16[16,256,128]{2,1,0:T(8,128)(2,1)}, bf16[2,16,2,128,128]{4,3,2,1,0:T(8,128)(2,1)S(1)}, bf16[16,2,128,128]{3,2,1,0:T(8,128)(2,1)S(1)}) custom-call(s32[1]{0:T(128)} %bitcast.parity_ref, bf16[256,2048]{1,0:T(8,128)(2,1)} %q_ref.1, bf16[256,2048]{1,0:T(8,128)(2,1)} %k_ref.1, bf16[256,2048]{1,0:T(8,128)(2,1)} %v_ref.1, ...), custom_call_target="tpu_custom_call" | custom-call | tf_op jit(solution)/shard_map/features/pallas_call | solution.py:140
  16.7 0.0 copy-start.2
  16.8 0.0 copy-start
  16.8 0.0 copy-start.1
  16.8 43.5 %conditional.1 = ((bf16[2,12,2,128,128]{4,3,2,1,0:T(8,128)(2,1)}, bf16[4,16,2,128,128]{4,3,2,1,0:T(8,128)(2,1)})) conditional(s32[]{:T(128)} %bitcast.2, (bf16[2,16,2,128,128]{4,3,2,1,0:T(8,128)(2,1)S(1)}, bf16[16,2,128,128]{3,2,1,0:T(8,128)(2,1)S(1)}) %tuple.98, (bf16[2,16,2,128,128]{4,3,2,1,0:T(8,128)(2,1)S(1)}, ...), branch_computations={%region_0.1_spmd, %region_1.2_spmd, %region_2.3_spmd, %region_3.4_... | conditional | bytes 8 | solution.py:563
  17.1 42.7 %exchange_25.1 = (bf16[2,12,2,128,128]{4,3,2,1,0:T(8,128)(2,1)}, bf16[4,16,2,128,128]{4,3,2,1,0:T(8,128)(2,1)}) custom-call(bf16[2,16,2,128,128]{4,3,2,1,0:T(8,128)(2,1)S(1)} %get-tuple-element.179.kv_ref, bf16[16,2,128,128]{3,2,1,0:T(8,128)(2,1)S(1)} %get-tuple-element.180.cand_ref), custom_call_target="tpu_custom_call" | custom-call | tf_op jit(solution)/shard_map/cond/branch_25_fun/exchange_25/pallas_call | solution.py:361
  60.3 0.0 copy-done.2
  60.3 0.1 constant_dynamic-slice_fusion
  60.4 0.1 copy.11
  60.5 0.0 copy-done
  60.5 0.0 copy-done.1
  60.5 20.7 %attention.1 = bf16[256,2048]{1,0:T(8,128)(2,1)S(1)} custom-call(f32[2,4]{1,0:T(2,128)S(1)} %compare_select_fusion.bias_ref, bf16[16,256,128]{2,1,0:T(8,128)(2,1)S(1)} %copy-done, bf16[2,16,2,128,128]{4,3,2,1,0:T(8,128)(2,1)S(1)} %get-tuple-element.197.kv_ref, bf16[2,12,2,128,128]{4,3,2,1,0:T(8,128)(2,1)} %get-tuple-element.199.early_in, ...), custom_call_target="tpu_custom_call" | custom-call | tf_op jit(solution)/shard_map/attention/pallas_call | solution.py:528
  81.3 1.0 %copy.75 = bf16[256,2048]{1,0:T(8,128)(2,1)} copy(bf16[256,2048]{1,0:T(8,128)(2,1)S(1)} %attention.1) | data formatting | bytes 2097152
  (2 shorter events, 0.0 us)
Async XLA Ops:
  16.7 43.6 %copy-start.2 = (s32[256,7]{0,1:T(8,128)S(1)}, s32[256,7]{0,1:T(8,128)}, u32[]{:S(2)}) copy-start(s32[256,7]{0,1:T(8,128)} %param.46) | copy-start | bytes 21508
  16.8 43.8 %copy-start = (bf16[16,256,128]{2,1,0:T(8,128)(2,1)S(1)}, bf16[16,256,128]{2,1,0:T(8,128)(2,1)}, u32[]{:S(2)}) copy-start(bf16[16,256,128]{2,1,0:T(8,128)(2,1)} %get-tuple-element.196.q_ref) | copy-start | bytes 3145732
  16.8 43.8 %copy-start.1 = (f32[2048]{0:T(1024)S(1)}, f32[2048]{0:T(1024)}, u32[]{:S(2)}) copy-start(f32[2048]{0:T(1024)} %param.45) | copy-start | bytes 24580
where the time goes:
time: 82.4 us; the launch traced here: 82.3 us
  Pallas kernels  77.6 us (94%)
  local copies, waits for them, and re-layouts  2.43 us (3%)
  between operations  1.37 us (2%)
  loops' own time  0.85 us (1%)
    pallas_call x1, Pallas kernels, exchange(): pl.pallas_call(functools.partial(exchange_kernel, source), out_shape=(jax...  42.7 us
    pallas_call x1, Pallas kernels, attention(): pl.pallas_call(attention_kernel, out_shape=jax.ShapeDtypeStruct((ROWS, HE...  20.7 us
    pallas_call x1, Pallas kernels, features(): pl.pallas_call(features_kernel, out_shape=(jax.ShapeDtypeStruct((HEADS_HE...  14.2 us

commit v1 on v0

--- a/solution.py
+++ b/solution.py
@@ -182,11 +182,11 @@
     outer = (me + last + 2 * core) % (last + 1)
 
     barrier = pltpu.get_barrier_semaphore()
-    z_targets = {kind: at(y, x, (z + move) % 8, core) for kind, move in [(6, 7), (7, 1), (8, 5), (9, 2)]}
-    z_others = [at(y, x, (z + move) % 8, core) for move in (1, 7, 3, 5, 2, 6)]
+    z_targets = {kind: at(y, x, (z + move) % 8, core) for kind, move in [(0, 7), (2, 5)]}
+    z_others = [at(y, x, (z + move) % 8, core) for move in (1, 7, 3, 5)]
     for other in z_others + [x_other, y_up, y_down, sibling, outer]:
         pl.semaphore_signal(barrier, inc=1, device_id={"ctx": other}, device_id_type=MESH)
-    pl.semaphore_wait(barrier, 11)
+    pl.semaphore_wait(barrier, 9)
 
     def band_copy(b):
         return pltpu.make_async_remote_copy(
@@ -216,10 +216,8 @@
         plane = y == s
         along = plane & main
         z_routes = [
-            (8, along & (steps == 0), z_targets[8]),
-            (9, along & (steps == 0), z_targets[9]),
-            (6, along & ((steps == 0) | (steps == 1) | (steps == 3) | (steps == 6)), z_targets[6]),
-            (7, along & (steps == 6), z_targets[7]),
+            (2, along & ((steps == 0) | (steps == 3)), z_targets[2]),
+            (0, along & (steps != 2) & (steps != 5) & (steps != 7), z_targets[0]),
         ]
         over_x = plane & (
             (main & jnp.logical_not((core == 1) & (steps == 0)))
@@ -245,10 +243,10 @@
         share = needs & jnp.logical_not(near_owner)
         routes = []
         if s < 3:
-            routes += [(2, up, y_up)]
+            routes += [(3, up, y_up)]
         if s < 2:
-            routes += [(3, down, y_down)]
-        routes = z_routes + [(1, over_x, x_other)] + routes + [(4, share, sibling)]
+            routes += [(4, down, y_down)]
+        routes = z_routes + [(1, over_x, x_other)] + routes + [(5, share, sibling)]
         depth = [
             jnp.where(y == 0, 0, jnp.where(y == 2, 2, 1)),
             jnp.where(y == 1, 0, jnp.where(y == 3, 2, 1)),
@@ -314,8 +312,8 @@
             @pl.when(owner & turn)
             def _():
                 h = theirs + j * GROUP
-                send(s, h, 5, sibling).wait_recv()
-                send(s, h, 5, sibling).start()
+                send(s, h, 6, sibling).wait_recv()
+                send(s, h, 6, sibling).start()
 
     for s in range(NGLOB):
         needs, owner, holds, routes, lag = plans[s]
@@ -328,7 +326,7 @@
 
         @pl.when(owner)
         def _():
-            sent(s, 5, theirs).wait_send()
+            sent(s, 6, theirs).wait_send()
 
         for kind, on, target in routes:
 
@@ -367,7 +365,7 @@
         in_specs=[vm, vm],
         out_specs=(hbm, hbm),
         scratch_shapes=[
-            pltpu.SemaphoreType.DMA((NGLOB, 10)),
+            pltpu.SemaphoreType.DMA((NGLOB, 7)),
             pltpu.SemaphoreType.DMA((NGLOB, HEADS_HERE)),
             pltpu.SemaphoreType.DMA((2,)),
             pltpu.SemaphoreType.DMA((2,)),

time: 82.4 us -> 81.5 us (0.989)
  no operation moved by 1% of the time
where the time goes in v1:
time: 81.5 us; the launch traced here: 81.3 us
  Pallas kernels  77.3 us (95%)
  local copies, waits for them, and re-layouts  2.43 us (3%)
  between operations  1.37 us (2%)
    pallas_call x1, Pallas kernels, exchange(): pl.pallas_call(functools.partial(exchange_kernel, source), out_shape=(jax...  42.6 us
    pallas_call x1, Pallas kernels, attention(): pl.pallas_call(attention_kernel, out_shape=jax.ShapeDtypeStruct((ROWS, HE...  20.5 us
    pallas_call x1, Pallas kernels, features(): pl.pallas_call(features_kernel, out_shape=(jax.ShapeDtypeStruct((HEADS_HE...  14.2 us

profile of v1, /device:TPU:24, one launch (start us, length us, event | category | flops | bytes accessed | tf_op | source)
XLA Modules:
  0.0 81.3 jit_solution(12166192826040633315)
XLA Ops:
  0.0 1.3 %slice.7 = s32[1,1]{0,1:T(1,128)} slice(s32[256,7]{0,1:T(8,128)} %param.46), slice={[255:256], [3:4]} | slice | bytes 8 | tf_op jit(solution)/shard_map/slice | solution.py:553
  1.9 14.2 %features.1 = (bf16[16,256,128]{2,1,0:T(8,128)(2,1)}, bf16[2,16,2,128,128]{4,3,2,1,0:T(8,128)(2,1)S(1)}, bf16[16,2,128,128]{3,2,1,0:T(8,128)(2,1)S(1)}) custom-call(s32[1]{0:T(128)} %bitcast.parity_ref, bf16[256,2048]{1,0:T(8,128)(2,1)} %q_ref.1, bf16[256,2048]{1,0:T(8,128)(2,1)} %k_ref.1, bf16[256,2048]{1,0:T(8,128)(2,1)} %v_ref.1, ...), custom_call_target="tpu_custom_call" | custom-call | tf_op jit(solution)/shard_map/features/pallas_call | solution.py:140
  16.7 0.0 copy-start.2
  16.8 0.0 copy-start
  16.8 0.0 copy-start.1
  16.8 42.8 %conditional.1 = ((bf16[2,12,2,128,128]{4,3,2,1,0:T(8,128)(2,1)}, bf16[4,16,2,128,128]{4,3,2,1,0:T(8,128)(2,1)})) conditional(s32[]{:T(128)} %bitcast.2, (bf16[2,16,2,128,128]{4,3,2,1,0:T(8,128)(2,1)S(1)}, bf16[16,2,128,128]{3,2,1,0:T(8,128)(2,1)S(1)}) %tuple.98, (bf16[2,16,2,128,128]{4,3,2,1,0:T(8,128)(2,1)S(1)}, ...), branch_computations={%region_0.1_spmd, %region_1.2_spmd, %region_2.3_spmd, %region_3.4_... | conditional | bytes 8 | solution.py:561
  16.8 42.6 %exchange_5.1 = (bf16[2,12,2,128,128]{4,3,2,1,0:T(8,128)(2,1)}, bf16[4,16,2,128,128]{4,3,2,1,0:T(8,128)(2,1)}) custom-call(bf16[2,16,2,128,128]{4,3,2,1,0:T(8,128)(2,1)S(1)} %get-tuple-element.139.kv_ref, bf16[16,2,128,128]{3,2,1,0:T(8,128)(2,1)S(1)} %get-tuple-element.140.cand_ref), custom_call_target="tpu_custom_call" | custom-call | tf_op jit(solution)/shard_map/cond/branch_5_fun/exchange_5/pallas_call | solution.py:359
  59.6 0.0 copy-done.2
  59.6 0.1 constant_dynamic-slice_fusion
  59.7 0.1 copy.11
  59.8 0.0 copy-done
  59.8 0.0 copy-done.1
  59.8 20.5 %attention.1 = bf16[256,2048]{1,0:T(8,128)(2,1)S(1)} custom-call(f32[2,4]{1,0:T(2,128)S(1)} %compare_select_fusion.bias_ref, bf16[16,256,128]{2,1,0:T(8,128)(2,1)S(1)} %copy-done, bf16[2,16,2,128,128]{4,3,2,1,0:T(8,128)(2,1)S(1)} %get-tuple-element.197.kv_ref, bf16[2,12,2,128,128]{4,3,2,1,0:T(8,128)(2,1)} %get-tuple-element.199.early_in, ...), custom_call_target="tpu_custom_call" | custom-call | tf_op jit(solution)/shard_map/attention/pallas_call | solution.py:526
  80.4 1.0 %copy.75 = bf16[256,2048]{1,0:T(8,128)(2,1)} copy(bf16[256,2048]{1,0:T(8,128)(2,1)S(1)} %attention.1) | data formatting | bytes 2097152
  (2 shorter events, 0.0 us)
Async XLA Ops:
  16.7 42.9 %copy-start.2 = (s32[256,7]{0,1:T(8,128)S(1)}, s32[256,7]{0,1:T(8,128)}, u32[]{:S(2)}) copy-start(s32[256,7]{0,1:T(8,128)} %param.46) | copy-start | bytes 21508
  16.8 43.0 %copy-start = (bf16[16,256,128]{2,1,0:T(8,128)(2,1)S(1)}, bf16[16,256,128]{2,1,0:T(8,128)(2,1)}, u32[]{:S(2)}) copy-start(bf16[16,256,128]{2,1,0:T(8,128)(2,1)} %get-tuple-element.196.q_ref) | copy-start | bytes 3145732
  16.8 43.0 %copy-start.1 = (f32[2048]{0:T(1024)S(1)}, f32[2048]{0:T(1024)}, u32[]{:S(2)}) copy-start(f32[2048]{0:T(1024)} %param.45) | copy-start | bytes 24580
